TPU v7x, 512 devices: a whole 4x8x8 slice. The times are simulated.
512 devices in a mesh: tm: 32 (over z, x), rows: 16 (over y, core).
Axes of the slice: x: 4, y: 8, z: 8, core: 2. Of those that a mesh axis runs over, the one named last changes fastest.
Arguments:
- frames: bfloat16 [64, 128, 48, 128], P('tm', 'rows'), may hold values from -60 to 60
- lengths: int32 [8], replicated, may hold values from 1 to 16, as said below
- norm_gain_one: float32 [128], replicated, may hold values from 0.5 to 1.5
- norm_shift_one: float32 [128], replicated, may hold values from -0.5 to 0.5
- conv_one: bfloat16 [3, 3, 3, 128, 128], replicated, may hold values from -0.109375 to 0.109375
- bias_one: float32 [128], replicated, may hold values from -1 to 1
- norm_gain_two: float32 [128], replicated, may hold values from 0.5 to 1.5
- norm_shift_two: float32 [128], replicated, may hold values from -0.5 to 0.5
- conv_two: bfloat16 [3, 3, 3, 128, 128], replicated, may hold values from -0.109375 to 0.109375
- bias_two: float32 [128], replicated, may hold values from -1 to 1
Outputs:
- encoded: float32 [64, 128, 48, 128], P('tm', 'rows')
Inputs may be any that keep to these rules, and one draw needn't show every extreme that they name: 8 video lengths that sum to 64; the longest has exactly 16 frames.
All inputs are finite; a program needn't handle non-finite values.
Results may differ from a plain program's by a relative error of at most 0.0014.
Values may be sent and summed in bfloat16 or wider, within the bound.
A program may use at most 64 MiB of HBM per device.

v0:
```python
import jax
import jax.numpy as jnp
from jax import lax
from jax.sharding import PartitionSpec as P

GROUPS = 32


def shifted(block, axis, distance):
    devices = range(lax.axis_size(axis))
    route = [(i - distance, i) for i in devices if i - distance in devices]
    return lax.ppermute(block, axis, route)


def extended(cells, sides, width):
    for axis, dim in sides:
        count = lax.axis_size(axis)
        ends = count - 1
        head = lax.slice_in_dim(cells, 0, width, axis=dim)
        tail = lax.slice_in_dim(cells, cells.shape[dim] - width, cells.shape[dim], axis=dim)
        cells = jnp.concatenate(
            [
                lax.ppermute(tail, axis, [(i, (i + 1) % count) for i in range(ends)]),
                cells,
                lax.ppermute(head, axis, [((i + 1) % count, i) for i in range(ends)]),
            ],
            axis=dim,
        )
    return cells


def plan_frames(lengths, count, first):
    videos = lengths.shape[0]
    offsets = jnp.cumsum(lengths) - lengths
    frame_ids = first + jnp.arange(count, dtype=jnp.int32)
    inside = offsets[None, :] <= frame_ids[:, None]
    video = jnp.sum(inside.astype(jnp.int32), axis=1) - 1
    starts = jnp.max(jnp.where(inside, offsets[None, :], 0), axis=1)
    onehot = (video[:, None] == jnp.arange(videos, dtype=jnp.int32)[None, :]).astype(jnp.float32)
    taps = [jnp.maximum(frame_ids - back, starts) - first + 2 for back in (2, 1, 0)]
    return (onehot, taps)


def group_totals(values):
    count = values.shape[0]
    width = values.shape[3]
    return jnp.sum(values, axis=(1, 2)).reshape(count, GROUPS, width // GROUPS).sum(-1)


def spread_groups(table, onehot, width):
    return jnp.repeat(
        jnp.dot(onehot, table, precision=lax.Precision.HIGHEST), width // GROUPS, axis=1
    )


def group_norm(values, onehot, counts, gain, shift):
    width = values.shape[3]
    sums = jnp.dot(onehot.T, group_totals(values), precision=lax.Precision.HIGHEST)
    mean = lax.psum(sums, ("tm", "rows")) / counts[:, None]
    centered = values - spread_groups(mean, onehot, width)[:, None, None, :]
    squares = jnp.dot(onehot.T, group_totals(centered * centered), precision=lax.Precision.HIGHEST)
    var = lax.psum(squares, ("tm", "rows")) / counts[:, None]
    scale = spread_groups(lax.rsqrt(var + 1e-06), onehot, width)
    return centered * scale[:, None, None, :] * gain + shift


def causal_conv(act, weight, bias, taps):
    count, height, cols_n, width = act.shape
    prior = shifted(act, "tm", 1)
    joined = jnp.concatenate([prior, act], axis=0)
    rimmed = extended(joined, (("rows", 1),), 1)
    padded = jnp.pad(rimmed, ((0, 0), (0, 0), (1, 1), (0, 0)))
    columns = jnp.concatenate(
        [padded[:, :, shift_col : shift_col + cols_n] for shift_col in range(3)], axis=-1
    )
    total = jnp.zeros((count * height * cols_n, width), jnp.float32)
    for step in range(3):
        picked = jnp.take(columns, taps[step], axis=0)
        for row_off in range(3):
            slab = picked[:, row_off : row_off + height].reshape(count * height * cols_n, 3 * width)
            kernel = weight[step, row_off].reshape(3 * width, width)
            total = total + jnp.dot(slab, kernel, preferred_element_type=jnp.float32)
    return total.reshape(count, height, cols_n, width) + bias


def per_device(
    frames,
    lengths,
    norm_gain_one,
    norm_shift_one,
    conv_one,
    bias_one,
    norm_gain_two,
    norm_shift_two,
    conv_two,
    bias_two,
):
    count, height, cols_n, width = frames.shape
    first = lax.axis_index("tm") * count
    onehot, taps = plan_frames(lengths, count, first)
    full_height = height * lax.axis_size("rows")
    counts = lengths.astype(jnp.float32) * (full_height * cols_n * (width // GROUPS))
    values = frames.astype(jnp.float32)
    act_one = jax.nn.silu(group_norm(values, onehot, counts, norm_gain_one, norm_shift_one)).astype(
        jnp.bfloat16
    )
    middle = causal_conv(act_one, conv_one, bias_one, taps).astype(jnp.bfloat16)
    act_two = jax.nn.silu(
        group_norm(middle.astype(jnp.float32), onehot, counts, norm_gain_two, norm_shift_two)
    ).astype(jnp.bfloat16)
    return values + causal_conv(act_two, conv_two, bias_two, taps)


def solution(mesh):
    placed = (P("tm", "rows", None, None), P(), P(), P(), P(), P(), P(), P(), P(), P())
    return jax.shard_map(
        per_device,
        mesh=mesh,
        in_specs=placed,
        out_specs=P("tm", "rows", None, None),
        check_vma=False,
    )
```

profile of v0, /device:TPU:89, one launch (start us, length us, event | category | flops | bytes accessed | tf_op | source)
XLA Modules:
  0.0 459.6 jit_solution(9391679192439192227)
XLA Ops:
  0.7 0.8 reduce-window.9
  2.4 1.0 convert_reduce_fusion
  3.9 101.7 %psum.28 = f32[8,32]{1,0:T(8,128)S(1)} all-reduce(f32[8,32]{1,0:T(8,128)S(1)} %fusion.56), channel_id=1, replica_groups=mesh['tm'=32,'rows'=16] {'tm','rows'}, use_global_device_ids=true, to_apply=%region_4.5 | all-reduce | flops 256 | bytes 2048 | tf_op jit(solution)/shard_map/psum | solution.py:59
  106.0 1.0 fusion.15
  107.5 94.3 %psum.29 = f32[8,32]{1,0:T(8,128)S(1)} all-reduce(f32[8,32]{1,0:T(8,128)S(1)} %fusion.55), channel_id=1, replica_groups=mesh['tm'=32,'rows'=16] {'tm','rows'}, use_global_device_ids=true, to_apply=%region_7.8 | all-reduce | flops 256 | bytes 2048 | tf_op jit(solution)/shard_map/psum | solution.py:62
  202.2 1.1 fusion.23
  203.3 3.7 collective-permute-start
  207.1 1.0 fusion.68
  208.1 5.6 %collective-permute-done = bf16[2,8,48,128]{3,2,1,0:T(8,128)(2,1)S(1)} collective-permute-done((bf16[2,8,48,128]{3,2,1,0:T(8,128)(2,1)S(1)}, bf16[2,8,48,128]{3,2,1,0:T(8,128)(2,1)S(1)}, u32[]{:S(2)}, u32[]{:S(2)}) %collective-permute-start) | collective-permute-done | bytes 196640 | tf_op jit(solution)/shard_map/ppermute | solution.py:12
  213.7 5.1 %collective-permute-start.1 = (bf16[4,1,48,128]{3,2,1,0:T(8,128)(2,1)S(1)}, bf16[4,1,48,128]{3,2,1,0:T(8,128)(2,1)S(1)}, u32[]{:S(2)}, u32[]{:S(2)}) collective-permute-start(bf16[4,1,48,128]{3,2,1,0:T(8,128)(2,1)S(1)} %get-tuple-element.58), channel_id=1, source_target_pairs={{0,1},{1,2},{2,3},{3,4},{4,5},{5,6},{6,7},{7,8},{8,9},{9,10},{10,1... | collective-permute-start | bytes 147464 | tf_op jit(solution)/shard_map/ppermute | solution.py:23
  218.8 1.9 collective-permute-start.2
  220.8 4.7 %collective-permute-done.2 = bf16[4,1,48,128]{3,2,1,0:T(8,128)(2,1)S(1)} collective-permute-done((bf16[4,1,48,128]{3,2,1,0:T(8,128)(2,1)S(1)}, bf16[4,1,48,128]{3,2,1,0:T(8,128)(2,1)S(1)}, u32[]{:S(2)}, u32[]{:S(2)}) %collective-permute-start.2) | collective-permute-done | bytes 49184 | tf_op jit(solution)/shard_map/ppermute | solution.py:25
  226.9 1.5 gather_fusion
  228.4 1.3 broadcast_select_fusion
  229.8 1.2 fusion.74
  237.2 94.4 %psum.30 = f32[8,32]{1,0:T(8,128)S(1)} all-reduce(f32[8,32]{1,0:T(8,128)S(1)} %fusion.54), channel_id=1, replica_groups=mesh['tm'=32,'rows'=16] {'tm','rows'}, use_global_device_ids=true, to_apply=%region_11.13 | all-reduce | flops 256 | bytes 2048 | tf_op jit(solution)/shard_map/psum | solution.py:59
  332.6 94.1 %psum.31 = f32[8,32]{1,0:T(8,128)S(1)} all-reduce(f32[8,32]{1,0:T(8,128)S(1)} %fusion.53), channel_id=1, replica_groups=mesh['tm'=32,'rows'=16] {'tm','rows'}, use_global_device_ids=true, to_apply=%region_14.16 | all-reduce | flops 256 | bytes 2048 | tf_op jit(solution)/shard_map/psum | solution.py:62
  427.2 2.8 collective-permute-start.3
  430.0 7.0 %collective-permute-done.3 = bf16[2,8,48,128]{3,2,1,0:T(8,128)(2,1)S(1)} collective-permute-done((bf16[2,8,48,128]{3,2,1,0:T(8,128)(2,1)S(1)}, bf16[2,8,48,128]{3,2,1,0:T(8,128)(2,1)S(1)}, u32[]{:S(2)}, u32[]{:S(2)}) %collective-permute-start.3) | collective-permute-done | bytes 196640 | tf_op jit(solution)/shard_map/ppermute | solution.py:12
  437.0 5.1 %collective-permute-start.4 = (bf16[4,1,48,128]{3,2,1,0:T(8,128)(2,1)S(1)}, bf16[4,1,48,128]{3,2,1,0:T(8,128)(2,1)S(1)}, u32[]{:S(2)}, u32[]{:S(2)}) collective-permute-start(bf16[4,1,48,128]{3,2,1,0:T(8,128)(2,1)S(1)} %get-tuple-element.56), channel_id=1, source_target_pairs={{0,1},{1,2},{2,3},{3,4},{4,5},{5,6},{6,7},{7,8},{8,9},{9,10},{10,1... | collective-permute-start | bytes 147464 | tf_op jit(solution)/shard_map/ppermute | solution.py:23
  442.1 2.1 collective-permute-start.5
  444.9 3.7 collective-permute-done.5
  449.4 1.5 gather_fusion.3
  452.4 1.3 broadcast_select_fusion.1
  (136 shorter events, 20.9 us)
Async XLA Ops:
  0.0 207.1 %copy-start.3 = (bf16[3,3,3,128,128]{4,3,2,1,0:T(8,128)(2,1)S(1)}, bf16[3,3,3,128,128]{4,3,2,1,0:T(8,128)(2,1)}, u32[]{:S(2)}) copy-start(bf16[3,3,3,128,128]{4,3,2,1,0:T(8,128)(2,1)} %param.16) | copy-start | bytes 2654212
  0.7 207.3 %copy-start.25 = (f32[8]{0:T(128)}, f32[8]{0:T(128)S(1)}, u32[]{:S(2)}) copy-start(f32[8]{0:T(128)S(1)} %convert_multiply_fusion) | copy-start | bytes 100
  2.4 205.6 %copy-start.27 = (s32[2]{0:T(128)}, s32[2]{0:T(128)S(1)}, u32[]{:S(2)}) copy-start(s32[2]{0:T(128)S(1)} %broadcast_add_fusion) | copy-start | bytes 28
  203.3 10.4 %collective-permute-start = (bf16[2,8,48,128]{3,2,1,0:T(8,128)(2,1)S(1)}, bf16[2,8,48,128]{3,2,1,0:T(8,128)(2,1)S(1)}, u32[]{:S(2)}, u32[]{:S(2)}) collective-permute-start(bf16[2,8,48,128]{3,2,1,0:T(8,128)(2,1)S(1)} %fusion.23), channel_id=1, source_target_pairs={{0,16},{16,32},{32,48},{48,64},{64,80},{80,96},{96,112},{112,128},... | collective-permute-start | bytes 589832 | tf_op jit(solution)/shard_map/ppermute | solution.py:12
  207.0 21.4 %copy-start.17 = (pred[2]{0:T(512)(128)(4,1)}, pred[2]{0:T(512)(128)(4,1)S(1)}, u32[]{:S(2)}) copy-start(pred[2]{0:T(512)(128)(4,1)S(1)} %get-tuple-element.10) | copy-start | bytes 10
  207.0 21.4 %copy-start.19 = (pred[2]{0:T(512)(128)(4,1)}, pred[2]{0:T(512)(128)(4,1)S(1)}, u32[]{:S(2)}) copy-start(pred[2]{0:T(512)(128)(4,1)S(1)} %get-tuple-element.62) | copy-start | bytes 10
  213.7 7.1 %collective-permute-start.1 = (bf16[4,1,48,128]{3,2,1,0:T(8,128)(2,1)S(1)}, bf16[4,1,48,128]{3,2,1,0:T(8,128)(2,1)S(1)}, u32[]{:S(2)}, u32[]{:S(2)}) collective-permute-start(bf16[4,1,48,128]{3,2,1,0:T(8,128)(2,1)S(1)} %get-tuple-element.58), channel_id=1, source_target_pairs={{0,1},{1,2},{2,3},{3,4},{4,5},{5,6},{6,7},{7,8},{8,9},{9,10},{10,1... | collective-permute-start | bytes 147464 | tf_op jit(solution)/shard_map/ppermute | solution.py:23
  218.8 6.6 %collective-permute-start.2 = (bf16[4,1,48,128]{3,2,1,0:T(8,128)(2,1)S(1)}, bf16[4,1,48,128]{3,2,1,0:T(8,128)(2,1)S(1)}, u32[]{:S(2)}, u32[]{:S(2)}) collective-permute-start(bf16[4,1,48,128]{3,2,1,0:T(8,128)(2,1)S(1)} %get-tuple-element.59), channel_id=1, source_target_pairs={{1,0},{2,1},{3,2},{4,3},{5,4},{6,5},{7,6},{8,7},{9,8},{10,9},{11,1... | collective-permute-start | bytes 147464 | tf_op jit(solution)/shard_map/ppermute | solution.py:25
  232.0 1.2 copy-start.2
  232.0 1.2 copy-start.12
  232.2 1.4 copy-start.1
  232.2 1.4 copy-start.11
  233.3 0.9 copy-start.10
  236.0 1.0 copy-start.28
  236.3 95.3 %copy-start.26 = (f32[8]{0:T(128)S(1)}, f32[8]{0:T(128)}, u32[]{:S(2)}) copy-start(f32[8]{0:T(128)} %copy-done.25) | copy-start | bytes 100
  236.3 190.7 %copy-start.22 = (f32[128]{0:T(128)S(1)}, f32[128]{0:T(128)}, u32[]{:S(2)}) copy-start(f32[128]{0:T(128)} %param.19) | copy-start | bytes 1540
  236.3 190.7 %copy-start.23 = (f32[128]{0:T(128)S(1)}, f32[128]{0:T(128)}, u32[]{:S(2)}) copy-start(f32[128]{0:T(128)} %param.18) | copy-start | bytes 1540
  236.7 207.5 %copy-start.4 = (bf16[3,3,3,128,128]{4,3,2,1,0:T(8,128)(2,1)S(1)}, bf16[3,3,3,128,128]{4,3,2,1,0:T(8,128)(2,1)}, u32[]{:S(2)}) copy-start(bf16[3,3,3,128,128]{4,3,2,1,0:T(8,128)(2,1)} %param.20) | copy-start | bytes 2654212
  427.2 9.8 %collective-permute-start.3 = (bf16[2,8,48,128]{3,2,1,0:T(8,128)(2,1)S(1)}, bf16[2,8,48,128]{3,2,1,0:T(8,128)(2,1)S(1)}, u32[]{:S(2)}, u32[]{:S(2)}) collective-permute-start(bf16[2,8,48,128]{3,2,1,0:T(8,128)(2,1)S(1)} %fusion.32), channel_id=1, source_target_pairs={{0,16},{16,32},{32,48},{48,64},{64,80},{80,96},{96,112},{112,128},... | collective-permute-start | bytes 589832 | tf_op jit(solution)/shard_map/ppermute | solution.py:12
  437.0 8.0 %collective-permute-start.4 = (bf16[4,1,48,128]{3,2,1,0:T(8,128)(2,1)S(1)}, bf16[4,1,48,128]{3,2,1,0:T(8,128)(2,1)S(1)}, u32[]{:S(2)}, u32[]{:S(2)}) collective-permute-start(bf16[4,1,48,128]{3,2,1,0:T(8,128)(2,1)S(1)} %get-tuple-element.56), channel_id=1, source_target_pairs={{0,1},{1,2},{2,3},{3,4},{4,5},{5,6},{6,7},{7,8},{8,9},{9,10},{10,1... | collective-permute-start | bytes 147464 | tf_op jit(solution)/shard_map/ppermute | solution.py:23
  442.1 6.6 %collective-permute-start.5 = (bf16[4,1,48,128]{3,2,1,0:T(8,128)(2,1)S(1)}, bf16[4,1,48,128]{3,2,1,0:T(8,128)(2,1)S(1)}, u32[]{:S(2)}, u32[]{:S(2)}) collective-permute-start(bf16[4,1,48,128]{3,2,1,0:T(8,128)(2,1)S(1)} %get-tuple-element.57), channel_id=1, source_target_pairs={{1,0},{2,1},{3,2},{4,3},{5,4},{6,5},{7,6},{8,7},{9,8},{10,9},{11,1... | collective-permute-start | bytes 147464 | tf_op jit(solution)/shard_map/ppermute | solution.py:25
  450.9 1.4 copy-start.20
  454.7 1.2 copy-start.15
  454.9 1.4 copy-start.14
  (11 other events, 9.5 us)
where the time goes:
time: 460 us
  blocking collectives  385 us (84%)
  waiting for transfers between devices  21 us (5%)
  starting transfers between devices  20.7 us (4%)
  local copies, waits for them, and re-layouts  14.3 us (3%)
  other arithmetic  11 us (2%)
  matrix products  7.45 us (2%)
    psum x2, blocking collectives, group_norm(): mean = lax.psum(sums, ('tm', 'rows')) / counts[:, None]  196 us
    psum x2, blocking collectives, group_norm(): var = lax.psum(squares, ('tm', 'rows')) / counts[:, None]  188 us
    ppermute x2, waiting for transfers between devices, shifted(): return lax.ppermute(block, axis, route)  12.6 us
    ppermute x2, starting transfers between devices, extended(): lax.ppermute(tail, axis, [(i, (i + 1) % count) for i in range(ends)])  10.2 us
  transfers between devices with their start and end apart: 6, of which 4 were waited for; matrix products, arithmetic and copies ran while one was open for 0% of the time, Pallas kernels for 0%

commit v1 on v0

--- a/solution.py
+++ b/solution.py
@@ -56,7 +56,7 @@
 def group_norm(values, onehot, counts, gain, shift):
     width = values.shape[3]
     sums = jnp.dot(onehot.T, group_totals(values), precision=lax.Precision.HIGHEST)
-    mean = lax.psum(sums, ("tm", "rows")) / counts[:, None]
+    mean = jax.lax.psum(jax.lax.psum(sums, axis_name="tm"), axis_name="rows") / counts[:, None]
     centered = values - spread_groups(mean, onehot, width)[:, None, None, :]
     squares = jnp.dot(onehot.T, group_totals(centered * centered), precision=lax.Precision.HIGHEST)
     var = lax.psum(squares, ("tm", "rows")) / counts[:, None]

time: 460 us -> 458 us (level)
  the two profiles are of different devices: /device:TPU:89 before, /device:TPU:27 now
where the time goes in v1:
time: 458 us; the launch traced here: 457 us
  blocking collectives  387 us (84%)
  waiting for transfers between devices  18.8 us (4%)
  starting transfers between devices  17.5 us (4%)
  local copies, waits for them, and re-layouts  14.3 us (3%)
  other arithmetic  11 us (2%)
  matrix products  7.45 us (2%)
    psum x2, blocking collectives, group_norm(): var = lax.psum(squares, ('tm', 'rows')) / counts[:, None]  198 us
    psum x2, blocking collectives, group_norm(): jax.lax.psum(sums, axis_name='tm')  118 us
    psum x2, blocking collectives, group_norm(): jax.lax.psum(jax.lax.psum(sums, axis_name='tm'), axis_name='rows')  71.3 us
    ppermute x2, waiting for transfers between devices, shifted(): return lax.ppermute(block, axis, route)  10.4 us
    ppermute x2, starting transfers between devices, extended(): lax.ppermute(tail, axis, [(i, (i + 1) % count) for i in range(ends)])  9.65 us
  transfers between devices with their start and end apart: 6, of which 4 were waited for; matrix products, arithmetic and copies ran while one was open for 0% of the time, Pallas kernels for 0%

profile of v1, /device:TPU:27, one launch (start us, length us, event | category | flops | bytes accessed | tf_op | source)
XLA Modules:
  0.0 456.9 jit_solution(12541542253429955449)
XLA Ops:
  2.4 1.0 convert_reduce_fusion
  3.9 62.9 %psum.42 = f32[8,32]{1,0:T(8,128)S(1)} all-reduce(f32[8,32]{1,0:T(8,128)S(1)} %fusion.56), channel_id=1, replica_groups=mesh['tm'=32,'rows'=16] {'tm'}, use_global_device_ids=true, to_apply=%region_4.5 | all-reduce | flops 256 | bytes 2048 | tf_op jit(solution)/shard_map/psum | solution.py:59
  66.8 37.1 %psum.43 = f32[8,32]{1,0:T(8,128)S(1)} all-reduce(f32[8,32]{1,0:T(8,128)S(1)} %psum.42), channel_id=1, replica_groups=mesh['tm'=32,'rows'=16] {'rows'}, use_global_device_ids=true, to_apply=%region_5.6 | all-reduce | flops 256 | bytes 2048 | tf_op jit(solution)/shard_map/psum | solution.py:59
  104.3 1.0 fusion.15
  105.7 99.5 %psum.44 = f32[8,32]{1,0:T(8,128)S(1)} all-reduce(f32[8,32]{1,0:T(8,128)S(1)} %fusion.55), channel_id=1, replica_groups=mesh['tm'=32,'rows'=16] {'tm','rows'}, use_global_device_ids=true, to_apply=%region_8.9 | all-reduce | flops 256 | bytes 2048 | tf_op jit(solution)/shard_map/psum | solution.py:62
  205.7 1.1 fusion.23
  206.8 1.9 collective-permute-start
  209.7 4.7 %collective-permute-done = bf16[2,8,48,128]{3,2,1,0:T(8,128)(2,1)S(1)} collective-permute-done((bf16[2,8,48,128]{3,2,1,0:T(8,128)(2,1)S(1)}, bf16[2,8,48,128]{3,2,1,0:T(8,128)(2,1)S(1)}, u32[]{:S(2)}, u32[]{:S(2)}) %collective-permute-start) | collective-permute-done | bytes 196640 | tf_op jit(solution)/shard_map/ppermute | solution.py:12
  214.4 4.8 %collective-permute-start.1 = (bf16[4,1,48,128]{3,2,1,0:T(8,128)(2,1)S(1)}, bf16[4,1,48,128]{3,2,1,0:T(8,128)(2,1)S(1)}, u32[]{:S(2)}, u32[]{:S(2)}) collective-permute-start(bf16[4,1,48,128]{3,2,1,0:T(8,128)(2,1)S(1)} %get-tuple-element.58), channel_id=1, source_target_pairs={{0,1},{1,2},{2,3},{3,4},{4,5},{5,6},{6,7},{7,8},{8,9},{9,10},{10,1... | collective-permute-start | bytes 147464 | tf_op jit(solution)/shard_map/ppermute | solution.py:23
  219.3 1.9 collective-permute-start.2
  221.2 4.7 %collective-permute-done.2 = bf16[4,1,48,128]{3,2,1,0:T(8,128)(2,1)S(1)} collective-permute-done((bf16[4,1,48,128]{3,2,1,0:T(8,128)(2,1)S(1)}, bf16[4,1,48,128]{3,2,1,0:T(8,128)(2,1)S(1)}, u32[]{:S(2)}, u32[]{:S(2)}) %collective-permute-start.2) | collective-permute-done | bytes 49184 | tf_op jit(solution)/shard_map/ppermute | solution.py:25
  227.3 1.5 gather_fusion
  228.9 1.3 broadcast_select_fusion
  230.2 1.2 fusion.74
  237.6 55.1 %psum.45 = f32[8,32]{1,0:T(8,128)S(1)} all-reduce(f32[8,32]{1,0:T(8,128)S(1)} %fusion.54), channel_id=1, replica_groups=mesh['tm'=32,'rows'=16] {'tm'}, use_global_device_ids=true, to_apply=%region_12.14 | all-reduce | flops 256 | bytes 2048 | tf_op jit(solution)/shard_map/psum | solution.py:59
  292.7 34.2 %psum.46 = f32[8,32]{1,0:T(8,128)S(1)} all-reduce(f32[8,32]{1,0:T(8,128)S(1)} %psum.45), channel_id=1, replica_groups=mesh['tm'=32,'rows'=16] {'rows'}, use_global_device_ids=true, to_apply=%region_13.15 | all-reduce | flops 256 | bytes 2048 | tf_op jit(solution)/shard_map/psum | solution.py:59
  327.8 98.4 %psum.47 = f32[8,32]{1,0:T(8,128)S(1)} all-reduce(f32[8,32]{1,0:T(8,128)S(1)} %fusion.53), channel_id=1, replica_groups=mesh['tm'=32,'rows'=16] {'tm','rows'}, use_global_device_ids=true, to_apply=%region_16.18 | all-reduce | flops 256 | bytes 2048 | tf_op jit(solution)/shard_map/psum | solution.py:62
  426.8 1.9 collective-permute-start.3
  428.7 5.7 %collective-permute-done.3 = bf16[2,8,48,128]{3,2,1,0:T(8,128)(2,1)S(1)} collective-permute-done((bf16[2,8,48,128]{3,2,1,0:T(8,128)(2,1)S(1)}, bf16[2,8,48,128]{3,2,1,0:T(8,128)(2,1)S(1)}, u32[]{:S(2)}, u32[]{:S(2)}) %collective-permute-start.3) | collective-permute-done | bytes 196640 | tf_op jit(solution)/shard_map/ppermute | solution.py:12
  434.4 4.8 %collective-permute-start.4 = (bf16[4,1,48,128]{3,2,1,0:T(8,128)(2,1)S(1)}, bf16[4,1,48,128]{3,2,1,0:T(8,128)(2,1)S(1)}, u32[]{:S(2)}, u32[]{:S(2)}) collective-permute-start(bf16[4,1,48,128]{3,2,1,0:T(8,128)(2,1)S(1)} %get-tuple-element.56), channel_id=1, source_target_pairs={{0,1},{1,2},{2,3},{3,4},{4,5},{5,6},{6,7},{7,8},{8,9},{9,10},{10,1... | collective-permute-start | bytes 147464 | tf_op jit(solution)/shard_map/ppermute | solution.py:23
  439.3 2.1 collective-permute-start.5
  442.2 3.7 collective-permute-done.5
  446.6 1.5 gather_fusion.3
  449.6 1.3 broadcast_select_fusion.1
  (138 shorter events, 22.7 us)
Async XLA Ops:
  0.0 208.8 %copy-start.3 = (bf16[3,3,3,128,128]{4,3,2,1,0:T(8,128)(2,1)S(1)}, bf16[3,3,3,128,128]{4,3,2,1,0:T(8,128)(2,1)}, u32[]{:S(2)}) copy-start(bf16[3,3,3,128,128]{4,3,2,1,0:T(8,128)(2,1)} %param.16) | copy-start | bytes 2654212
  0.7 209.0 %copy-start.25 = (f32[8]{0:T(128)}, f32[8]{0:T(128)S(1)}, u32[]{:S(2)}) copy-start(f32[8]{0:T(128)S(1)} %convert_multiply_fusion) | copy-start | bytes 100
  2.4 207.3 %copy-start.27 = (s32[2]{0:T(128)}, s32[2]{0:T(128)S(1)}, u32[]{:S(2)}) copy-start(s32[2]{0:T(128)S(1)} %broadcast_add_fusion) | copy-start | bytes 28
  206.8 7.7 %collective-permute-start = (bf16[2,8,48,128]{3,2,1,0:T(8,128)(2,1)S(1)}, bf16[2,8,48,128]{3,2,1,0:T(8,128)(2,1)S(1)}, u32[]{:S(2)}, u32[]{:S(2)}) collective-permute-start(bf16[2,8,48,128]{3,2,1,0:T(8,128)(2,1)S(1)} %fusion.23), channel_id=1, source_target_pairs={{0,16},{16,32},{32,48},{48,64},{64,80},{80,96},{96,112},{112,128},... | collective-permute-start | bytes 589832 | tf_op jit(solution)/shard_map/ppermute | solution.py:12
  208.7 20.1 %copy-start.17 = (pred[2]{0:T(512)(128)(4,1)}, pred[2]{0:T(512)(128)(4,1)S(1)}, u32[]{:S(2)}) copy-start(pred[2]{0:T(512)(128)(4,1)S(1)} %get-tuple-element.10) | copy-start | bytes 10
  208.7 20.1 %copy-start.19 = (pred[2]{0:T(512)(128)(4,1)}, pred[2]{0:T(512)(128)(4,1)S(1)}, u32[]{:S(2)}) copy-start(pred[2]{0:T(512)(128)(4,1)S(1)} %get-tuple-element.62) | copy-start | bytes 10
  214.4 6.8 %collective-permute-start.1 = (bf16[4,1,48,128]{3,2,1,0:T(8,128)(2,1)S(1)}, bf16[4,1,48,128]{3,2,1,0:T(8,128)(2,1)S(1)}, u32[]{:S(2)}, u32[]{:S(2)}) collective-permute-start(bf16[4,1,48,128]{3,2,1,0:T(8,128)(2,1)S(1)} %get-tuple-element.58), channel_id=1, source_target_pairs={{0,1},{1,2},{2,3},{3,4},{4,5},{5,6},{6,7},{7,8},{8,9},{9,10},{10,1... | collective-permute-start | bytes 147464 | tf_op jit(solution)/shard_map/ppermute | solution.py:23
  219.3 6.6 %collective-permute-start.2 = (bf16[4,1,48,128]{3,2,1,0:T(8,128)(2,1)S(1)}, bf16[4,1,48,128]{3,2,1,0:T(8,128)(2,1)S(1)}, u32[]{:S(2)}, u32[]{:S(2)}) collective-permute-start(bf16[4,1,48,128]{3,2,1,0:T(8,128)(2,1)S(1)} %get-tuple-element.59), channel_id=1, source_target_pairs={{1,0},{2,1},{3,2},{4,3},{5,4},{6,5},{7,6},{8,7},{9,8},{10,9},{11,1... | collective-permute-start | bytes 147464 | tf_op jit(solution)/shard_map/ppermute | solution.py:25
  232.4 1.2 copy-start.2
  232.4 1.2 copy-start.12
  232.6 1.4 copy-start.1
  232.6 1.4 copy-start.11
  233.7 0.9 copy-start.10
  236.4 1.0 copy-start.28
  236.7 90.2 %copy-start.26 = (f32[8]{0:T(128)S(1)}, f32[8]{0:T(128)}, u32[]{:S(2)}) copy-start(f32[8]{0:T(128)} %copy-done.25) | copy-start | bytes 100
  236.7 189.9 %copy-start.22 = (f32[128]{0:T(128)S(1)}, f32[128]{0:T(128)}, u32[]{:S(2)}) copy-start(f32[128]{0:T(128)} %param.19) | copy-start | bytes 1540
  236.7 189.9 %copy-start.23 = (f32[128]{0:T(128)S(1)}, f32[128]{0:T(128)}, u32[]{:S(2)}) copy-start(f32[128]{0:T(128)} %param.18) | copy-start | bytes 1540
  237.1 204.3 %copy-start.4 = (bf16[3,3,3,128,128]{4,3,2,1,0:T(8,128)(2,1)S(1)}, bf16[3,3,3,128,128]{4,3,2,1,0:T(8,128)(2,1)}, u32[]{:S(2)}) copy-start(bf16[3,3,3,128,128]{4,3,2,1,0:T(8,128)(2,1)} %param.20) | copy-start | bytes 2654212
  426.8 7.7 %collective-permute-start.3 = (bf16[2,8,48,128]{3,2,1,0:T(8,128)(2,1)S(1)}, bf16[2,8,48,128]{3,2,1,0:T(8,128)(2,1)S(1)}, u32[]{:S(2)}, u32[]{:S(2)}) collective-permute-start(bf16[2,8,48,128]{3,2,1,0:T(8,128)(2,1)S(1)} %fusion.32), channel_id=1, source_target_pairs={{0,16},{16,32},{32,48},{48,64},{64,80},{80,96},{96,112},{112,128},... | collective-permute-start | bytes 589832 | tf_op jit(solution)/shard_map/ppermute | solution.py:12
  434.4 7.7 %collective-permute-start.4 = (bf16[4,1,48,128]{3,2,1,0:T(8,128)(2,1)S(1)}, bf16[4,1,48,128]{3,2,1,0:T(8,128)(2,1)S(1)}, u32[]{:S(2)}, u32[]{:S(2)}) collective-permute-start(bf16[4,1,48,128]{3,2,1,0:T(8,128)(2,1)S(1)} %get-tuple-element.56), channel_id=1, source_target_pairs={{0,1},{1,2},{2,3},{3,4},{4,5},{5,6},{6,7},{7,8},{8,9},{9,10},{10,1... | collective-permute-start | bytes 147464 | tf_op jit(solution)/shard_map/ppermute | solution.py:23
  439.3 6.6 %collective-permute-start.5 = (bf16[4,1,48,128]{3,2,1,0:T(8,128)(2,1)S(1)}, bf16[4,1,48,128]{3,2,1,0:T(8,128)(2,1)S(1)}, u32[]{:S(2)}, u32[]{:S(2)}) collective-permute-start(bf16[4,1,48,128]{3,2,1,0:T(8,128)(2,1)S(1)} %get-tuple-element.57), channel_id=1, source_target_pairs={{1,0},{2,1},{3,2},{4,3},{5,4},{6,5},{7,6},{8,7},{9,8},{10,9},{11,1... | collective-permute-start | bytes 147464 | tf_op jit(solution)/shard_map/ppermute | solution.py:25
  448.1 1.4 copy-start.20
  452.0 1.2 copy-start.15
  452.2 1.4 copy-start.14
  (11 other events, 9.6 us)
